TPU v7x, 256 devices: a whole 4x4x8 slice. The times are simulated.
256 devices in a mesh: dp: 16 (over z, core), tensor: 16 (over x, y).
Axes of the slice: x: 4, y: 4, z: 8, core: 2. Of those that a mesh axis runs over, the one named last changes fastest.
Arguments:
- grad_gate: bfloat16 [16, 28672, 256], P('dp', 'tensor'), may hold values from -6 to 6
- error_gate: float32 [16, 28672, 256], P('dp', 'tensor'), may hold values from -4 to 4
- query_gate: float32 [32, 256], replicated, may hold values from -6 to 6
- grad_down: bfloat16 [16, 256, 28672], P('dp', None, 'tensor'), may hold values from -6 to 6
- error_down: float32 [16, 256, 28672], P('dp', None, 'tensor'), may hold values from -4 to 4
- query_down: float32 [32, 28672], P(None, 'tensor'), may hold values from -6 to 6
Outputs:
- update_gate: float32 [28672, 256], P('tensor')
- new_error_gate: float32 [16, 28672, 256], P('dp', 'tensor')
- update_down: float32 [256, 28672], P(None, 'tensor')
- new_error_down: float32 [16, 256, 28672], P('dp', None, 'tensor')
All inputs are finite; a program needn't handle non-finite values.
Results may differ from a plain program's by a relative error of at most 0.0003.
Values sent between devices are 32-bit elements; how exact they have to be, the bound alone decides.
A program may use at most 64 MiB of HBM per device.

v0:
```python
import jax
import jax.numpy as jnp
from jax import lax
from jax.sharding import PartitionSpec as P

HIGH = lax.Precision.HIGHEST


def contract_last(left, right):
    return lax.dot_general(left, right, (((1,), (1,)), ((), ())), precision=HIGH)


def contract_first(left, right):
    return lax.dot_general(left, right, (((0,), (0,)), ((), ())), precision=HIGH)


def cholesky_rows(sketch, gram):
    lower = jnp.linalg.cholesky(gram)
    return lax.linalg.triangular_solve(lower, sketch, left_side=True, lower=True)


def local(grad_gate, error_gate, query_gate, grad_down, error_down, query_down):
    workers = lax.axis_size("dp")
    full_gate = grad_gate[0].astype(jnp.float32) + error_gate[0]
    full_down = grad_down[0].astype(jnp.float32) + error_down[0]
    part_gate = contract_last(query_gate, full_gate)
    part_down = contract_last(query_down, full_down)
    sketch_down = None
    sketch_gate = lax.psum(part_gate, "dp")
    gram = lax.psum(contract_last(sketch_gate, sketch_gate), "tensor")
    basis_gate = cholesky_rows(sketch_gate, gram)
    sketch_down = lax.psum(part_down, ("dp", "tensor"))
    basis_down = cholesky_rows(sketch_down, contract_last(sketch_down, sketch_down))
    local_gate = jnp.dot(basis_gate, full_gate, precision=HIGH)
    local_down = jnp.dot(basis_down, full_down, precision=HIGH)
    coeff_gate = lax.psum(local_gate, ("dp", "tensor")) / workers
    coeff_down = lax.psum(local_down, "dp") / workers
    update_gate = contract_first(basis_gate, coeff_gate)
    update_down = contract_first(basis_down, coeff_down)
    return (
        update_gate,
        (full_gate - update_gate)[None],
        update_down,
        (full_down - update_down)[None],
    )


def solution(mesh):
    in_specs = (
        P("dp", "tensor", None),
        P("dp", "tensor", None),
        P(),
        P("dp", None, "tensor"),
        P("dp", None, "tensor"),
        P(None, "tensor"),
    )
    out_specs = (
        P("tensor", None),
        P("dp", "tensor", None),
        P(None, "tensor"),
        P("dp", None, "tensor"),
    )
    return jax.shard_map(local, mesh=mesh, in_specs=in_specs, out_specs=out_specs, check_vma=False)
```

profile of v0, /device:TPU:1, one launch (start us, length us, event | category | flops | bytes accessed | tf_op | source)
XLA Modules:
  0.0 569.2 jit_solution(13907596832315506223)
XLA Ops:
  7.2 0.0 copy-start
  7.2 0.0 all-reduce.5.cloned.1.call-start
  7.2 4.4 convolution_bitcast_fusion
  11.6 0.0 all-reduce.5.cloned.1.call-update
  11.6 0.0 copy-start.1
  11.7 0.0 copy-start.3
  11.7 0.0 all-reduce.9.cloned.1.call-start
  11.7 0.0 copy-done
  11.7 4.2 fusion.9
  15.9 106.8 %all-reduce.5.cloned.1.call-done = f32[32,1792]{1,0:T(8,128)} async-done(((f32[32,1792]{1,0:T(8,128)}), f32[32,1792]{1,0:T(8,128)}) %all-reduce.5.cloned.1.call-update) | async-done | bytes 229392 | tf_op jit(solution)/shard_map/psum | solution.py:29
  122.7 1.4 fusion.28
  124.1 60.5 %psum.36 = f32[32,32]{0,1:T(8,128)S(1)} all-reduce(f32[32,32]{0,1:T(8,128)S(1)} %fusion.28), channel_id=1, replica_groups=mesh['dp'=16,'tensor'=16] {'tensor'}, use_global_device_ids=true, to_apply=%region_1.0 | all-reduce | flops 1024 | bytes 8192 | tf_op jit(solution)/shard_map/psum | solution.py:30
  184.6 0.1 copy.11
  184.7 2.9 cholesky.44
  187.6 0.6 compare_reduce_fusion.1
  188.2 0.7 fusion.17
  188.9 2.4 custom-call.8
  191.3 1.3 fusion.22
  192.7 0.0 copy-done.1
  192.7 0.0 copy-done.3
  192.7 1.7 fusion.5
  194.4 0.0 all-reduce.9.cloned.1.call-update
  194.4 0.0 all-reduce.7.cloned.1.call-start
  194.5 246.3 %all-reduce.9.cloned.1.call-done = (f32[32,256]{1,0:T(8,128)}, f32[32,256]{1,0:T(8,128)}) async-done(((f32[32,256]{1,0:T(8,128)}, f32[32,256]{1,0:T(8,128)}), (f32[32,256]{1,0:T(8,128)}, f32[32,256]{1,0:T(8,128)})) %all-reduce.9.cloned.1.call-update) | async-done | bytes 65552 | tf_op jit(solution)/shard_map/psum | solution.py:36
  440.7 0.0 copy-start.6
  440.7 1.0 fusion.29
  441.7 0.1 copy.12
  441.8 2.9 cholesky.55
  444.8 0.6 compare_reduce_fusion
  445.4 0.7 fusion.18
  446.1 2.4 custom-call.9
  448.5 1.0 fusion.19
  449.5 3.7 fusion
  453.2 0.0 all-reduce.7.cloned.1.call-update
  453.2 0.0 copy-done.6
  453.2 1.7 fusion.15
  454.9 0.0 copy-start.4
  454.9 1.2 copy-done.4
  456.1 1.5 fusion.8
  457.7 0.0 copy-start.2
  457.7 99.0 %all-reduce.7.cloned.1.call-done = f32[32,1792]{1,0:T(8,128)} async-done(((f32[32,1792]{1,0:T(8,128)}), f32[32,1792]{1,0:T(8,128)}) %all-reduce.7.cloned.1.call-update) | async-done | bytes 229392 | tf_op jit(solution)/shard_map/psum | solution.py:37
  556.7 2.6 fusion.12
  559.3 0.0 copy-done.2
  559.3 0.0 copy-start.5
  559.3 3.4 fusion.4
  562.7 0.0 copy-done.5
  (4 shorter events, 0.1 us)
Async XLA Ops:
  7.2 4.6 copy-start
  7.2 115.5 %all-reduce.5.cloned.1.call-start = ((), (), s32[]{:S(2)}) async-start(), calls=%async_computation | async-start | bytes 458752 | tf_op jit(solution)/shard_map/psum | solution.py:29
  11.6 181.1 %copy-start.1 = (f32[1,1792,256]{2,1,0:T(8,128)S(1)}, f32[1,1792,256]{2,1,0:T(8,128)}, u32[]{:S(2)}) copy-start(f32[1,1792,256]{2,1,0:T(8,128)} %param.8) | copy-start | bytes 5505028
  11.7 181.0 %copy-start.3 = (bf16[1,1792,256]{2,1,0:T(8,128)(2,1)S(1)}, bf16[1,1792,256]{2,1,0:T(8,128)(2,1)}, u32[]{:S(2)}) copy-start(bf16[1,1792,256]{2,1,0:T(8,128)(2,1)} %param.7) | copy-start | bytes 2752516
  11.7 429.1 %all-reduce.9.cloned.1.call-start = ((), (), s32[]{:S(2)}) async-start(), calls=%async_computation.2 | async-start | bytes 131072 | tf_op jit(solution)/shard_map/psum | solution.py:36
  194.4 362.3 %all-reduce.7.cloned.1.call-start = ((), (), s32[]{:S(2)}) async-start(), calls=%async_computation.1 | async-start | bytes 458752 | tf_op jit(solution)/shard_map/psum | solution.py:37
  440.7 12.5 %copy-start.6 = (f32[32,256]{1,0:T(8,128)S(1)}, f32[32,256]{1,0:T(8,128)}, u32[]{:S(2)}) copy-start(f32[32,256]{1,0:T(8,128)} %get-tuple-element.5) | copy-start | bytes 98308
  454.9 1.2 copy-start.4
  457.7 101.6 %copy-start.2 = (f32[1,256,1792]{2,1,0:T(8,128)S(1)}, f32[1,256,1792]{2,1,0:T(8,128)}, u32[]{:S(2)}) copy-start(f32[1,256,1792]{2,1,0:T(8,128)} %param.11) | copy-start | bytes 5505028
  559.3 3.4 copy-start.5
Sparse Core Ops, SparseCore 0:
  11.8 110.8 all-reduce.4
  194.5 246.1 all-reduce.8
  453.3 103.3 all-reduce.6
where the time goes:
time: 570 us; the launch traced here: 569 us
  waiting for transfers between devices  452 us (79%)
  blocking collectives  60.5 us (11%)
  matrix products  22.8 us (4%)
  other arithmetic  18.3 us (3%)
  between operations  13.9 us (2%)
    psum x1, waiting for transfers between devices, local(): coeff_gate = lax.psum(local_gate, ('dp', 'tensor')) / workers  246 us
    psum x1, waiting for transfers between devices, local(): sketch_gate = lax.psum(part_gate, 'dp')  107 us
    psum x1, waiting for transfers between devices, local(): coeff_down = lax.psum(local_down, 'dp') / workers  99 us
    psum x1, blocking collectives, local(): gram = lax.psum(contract_last(sketch_gate, sketch_gate), 'tensor')  60.5 us
  transfers between devices with their start and end apart: 3, of which 3 were waited for; matrix products, arithmetic and copies ran while one was open for 1% of the time, Pallas kernels for 0%

commit v1 on v0

v1 whole, which is shorter than its diff:
```python
import functools

import jax
import jax.numpy as jnp
from jax import lax
from jax.experimental import pallas as pl
from jax.experimental.pallas import tpu as pltpu
from jax.sharding import PartitionSpec as P

MESH = pl.DeviceIdType.MESH
F32, BF16 = jnp.float32, jnp.bfloat16
HIGH = lax.Precision.HIGHEST
NN = (((1,), (0,)), ((), ()))
NT = (((1,), (1,)), ((), ()))
TN = (((0,), (0,)), ((), ()))
LANES = 128
BLOCK = 256
RANK = 32
Z, XY = 8, 16
OWNERS = 7
Z_ORDER = (4, 3, 5, 2, 6, 1, 7)
XY_ORDER = sorted(
    ((dx, dy) for dx in range(4) for dy in range(4) if dx or dy),
    key=lambda o: -(min(o[0], 4 - o[0]) + min(o[1], 4 - o[1])),
)


def split3(x):
    hi = x.astype(BF16)
    rest = x - hi.astype(F32)
    mid = rest.astype(BF16)
    return hi, mid, (rest - mid.astype(F32)).astype(BF16)


def rows3(x):
    return jnp.concatenate(split3(x), axis=0)


def dot(a, b, dims):
    return lax.dot_general(a, b, dims, preferred_element_type=F32)


def dot_high(a, b, dims):
    return lax.dot_general(a, b, dims, precision=HIGH, preferred_element_type=F32)


def dot6(left3, right, dims):
    hi, mid, lo = right
    a = dot(left3, hi, dims)
    b = dot(left3[: 2 * RANK], mid, dims)
    c = dot(left3[:RANK], lo, dims)
    small = a[2 * RANK :] + b[RANK:] + c
    return a[:RANK] + ((a[RANK : 2 * RANK] + b[:RANK]) + small)


def total(ref, n):
    out = ref[0]
    for i in range(1, n):
        out = out + ref[i]
    return out


def eliminate(gram):
    rows = lax.broadcasted_iota(jnp.int32, (RANK, LANES), 0)
    lanes = lax.broadcasted_iota(jnp.int32, (RANK, LANES), 1)
    a = gram + (lanes == rows + RANK).astype(F32)
    index = lax.broadcasted_iota(jnp.int32, (RANK, 1), 0)
    inverse = jnp.zeros((RANK, 1), F32)
    for k in range(RANK):
        row = a[k : k + 1, :]
        inv = 1.0 / a[k : k + 1, k : k + 1]
        inverse = jnp.where(index == k, inv, inverse)
        column = a[:, k : k + 1]
        a = a - jnp.where(index > k, column * inv, 0.0) * row
    return a[:, RANK : 2 * RANK], inverse


def exchange_kernel(
    gg_hbm, eg_hbm, qg_hbm, gd_hbm, ed_hbm, qd_hbm,
    basis_g, coeff_g, basis_d, coeff_d,
    gg, eg, qg, gd, ed, qd, fg, fd,
    sg_part, sg_sib, sg_half, rs_g, sg,
    sfg, sfg_sib, msg_g, z1_g, x1_g, mid_g, z2_g, x2_g, full_g,
    sd_part, sd_sib, msg_d, z1_d, x1_d, mid_d, z2_d, x2_d, sd,
    sfd, sfd_sib, sfd_half, rs_d, own_g, own_d,
    load_sem, send_sem, recv_sem,
):
    dp, t = lax.axis_index("dp"), lax.axis_index("tensor")
    z, c = dp // 2, dp % 2
    x, y = t // 4, t % 4
    sibling = (dp + 1 - 2 * c, t)
    z_peers = [(lax.rem(z + i, Z), (2 * lax.rem(z + i, Z) + c, t)) for i in Z_ORDER]
    xy_peers = [(dp, lax.rem(x + dx, 4) * 4 + lax.rem(y + dy, 4)) for dx, dy in XY_ORDER]

    barrier = pltpu.get_barrier_semaphore()
    for device in [sibling] + [d for _, d in z_peers] + xy_peers:
        pl.semaphore_signal(barrier, inc=1, device_id=device, device_id_type=MESH)

    loads = [
        pltpu.make_async_copy(src, dst, load_sem.at[i])
        for i, (src, dst) in enumerate(
            ((qd_hbm, qd), (gd_hbm, gd), (ed_hbm, ed), (qg_hbm, qg), (gg_hbm, gg), (eg_hbm, eg))
        )
    ]
    for load in loads:
        load.start()

    def send(stage, src, dst, device):
        pltpu.make_async_remote_copy(
            src_ref=src, dst_ref=dst, send_sem=send_sem.at[stage], recv_sem=recv_sem.at[stage],
            device_id=device, device_id_type=MESH,
        ).start()

    def received(stage, ref):
        pltpu.make_async_copy(ref, ref, recv_sem.at[stage]).wait()

    def sent(stage, ref):
        pltpu.make_async_copy(ref, ref, send_sem.at[stage]).wait()

    blocks = gg.shape[0] // BLOCK
    for load in loads[:3]:
        load.wait()
    sd_sum = None
    for b in range(blocks):
        cols = pl.ds(b * BLOCK, BLOCK)
        parts = split3(gd[:, cols].astype(F32) + ed[:, cols])
        for i in range(3):
            fd[i, :, cols] = parts[i]
        term = dot6(rows3(qd[:, cols]), parts, NT)
        sd_sum = term if sd_sum is None else sd_sum + term
    sd_part[0] = sd_sum[:, :LANES]
    sd_part[1] = sd_sum[:, LANES:]
    for load in loads[3:]:
        load.wait()
    qg3 = rows3(qg[...])
    for b in range(blocks):
        rows = pl.ds(b * BLOCK, BLOCK)
        parts = split3(gg[rows, :].astype(F32) + eg[rows, :])
        for i in range(3):
            fg[i, rows, :] = parts[i]
        term = dot6(qg3, parts, NT)
        sg_part[2 * b] = term[:, :LANES]
        sg_part[2 * b + 1] = term[:, LANES:]

    pl.semaphore_wait(barrier, 1 + len(z_peers) + len(xy_peers))

    mine, other = OWNERS * c, OWNERS * (1 - c)
    send(0, sd_part.at[1 - c], sd_sib, sibling)
    send(1, sg_part.at[pl.ds(other, OWNERS)], sg_sib, sibling)

    def reduce_first(base, value, extra, msg, z1, x1):
        msg[0:32] = value
        if extra is not None:
            msg[32:40] = extra
        z1[z] = msg[0:16]
        high = msg.at[pl.ds(16, msg.shape[0] - 16)]
        x1[t] = high[...]
        for device in xy_peers:
            send(base + 1, high, x1.at[t], device)
        for _, device in z_peers:
            send(base, msg.at[pl.ds(0, 16)], z1.at[z], device)

    def reduce_second(base, z1, x1, mid, z2, x2):
        received(base, z1.at[pl.ds(0, Z - 1)])
        low = total(z1, Z)
        mid[0:16] = low
        x2[t] = low
        for device in xy_peers:
            send(base + 3, mid.at[pl.ds(0, 16)], x2.at[t], device)
        received(base + 1, x1.at[pl.ds(0, XY - 1)])
        high = total(x1, XY)
        mid[16:32] = high[0:16]
        z2[z] = high[0:16]
        for _, device in z_peers:
            send(base + 2, mid.at[pl.ds(16, 16)], z2.at[z], device)
        return high[16:]

    def reduce_third(base, z2, x2, full):
        received(base + 2, z2.at[pl.ds(0, Z - 1)])
        received(base + 3, x2.at[pl.ds(0, XY - 1)])
        full[c, 0:16] = total(x2, XY)
        full[c, 16:32] = total(z2, Z)
        send(base + 4, full.at[c], full.at[c], sibling)

    def scatter(stage, half, rs):
        for peer, device in z_peers:
            @pl.when(peer < OWNERS)
            def _():
                send(stage, half.at[peer], rs.at[z], device)

        @pl.when(z < OWNERS)
        def _():
            rs[z] = half[z]

    def gather(stage, own, dst):
        @pl.when(z < OWNERS)
        def _():
            dst[mine + z] = own[...]
            for _, device in z_peers:
                send(stage, own, dst.at[mine + z], device)

    def gathered(stage, dst):
        @pl.when(z < OWNERS)
        def _():
            received(stage, dst.at[pl.ds(0, OWNERS - 1)])

        @pl.when(z == OWNERS)
        def _():
            received(stage, dst.at[pl.ds(0, OWNERS)])

    received(0, sd_sib)
    reduce_first(2, sd_part[c] + sd_sib[...], None, msg_d, z1_d, x1_d)
    received(1, sg_sib)
    for i in range(OWNERS):
        sg_half[i] = sg_part[mine + i] + sg_sib[i]
    scatter(7, sg_half, rs_g)

    reduce_second(2, z1_d, x1_d, mid_d, z2_d, x2_d)

    @pl.when(z < OWNERS)
    def _():
        received(7, rs_g.at[pl.ds(0, Z - 1)])
        own_g[...] = total(rs_g, Z)

    gather(8, own_g, sg)

    reduce_third(2, z2_d, x2_d, sd)
    received(6, sd.at[1 - c])

    sketch_d = jnp.concatenate([sd[0], sd[1]], axis=1)
    sd3 = rows3(sketch_d)
    for b in range(blocks):
        cols = pl.ds(b * BLOCK, BLOCK)
        term = dot6(sd3, [fd[i, :, cols] for i in range(3)], NN)
        sfd[2 * b] = term[:, :LANES]
        sfd[2 * b + 1] = term[:, LANES:]
    send(9, sfd.at[pl.ds(other, OWNERS)], sfd_sib, sibling)

    gathered(8, sg)
    send(10, sg.at[pl.ds(mine, OWNERS)], sg.at[pl.ds(mine, OWNERS)], sibling)
    received(9, sfd_sib)
    for i in range(OWNERS):
        sfd_half[i] = sfd[mine + i] + sfd_sib[i]
    scatter(11, sfd_half, rs_d)

    received(10, sg.at[pl.ds(other, OWNERS)])
    sfg_sum = None
    gram_sum = None
    zeros = jnp.zeros((LANES - RANK, BLOCK), F32)
    for b in range(blocks):
        rows = pl.ds(b * BLOCK, BLOCK)
        tile = jnp.concatenate([sg[2 * b], sg[2 * b + 1]], axis=1)
        term = dot6(rows3(tile), [fg[i, rows, :] for i in range(3)], NN)
        sfg_sum = term if sfg_sum is None else sfg_sum + term
        term = dot_high(tile, jnp.concatenate([tile, zeros], axis=0), NT)
        gram_sum = term if gram_sum is None else gram_sum + term
    packed = gram_sum[0:8]
    for i in range(1, 4):
        packed = packed + pltpu.roll(gram_sum[8 * i : 8 * i + 8], RANK * i, 1)
    sfg[0] = sfg_sum[:, :LANES]
    sfg[1] = sfg_sum[:, LANES:]
    send(12, sfg.at[1 - c], sfg_sib, sibling)

    pad = jnp.zeros((LANES - RANK, BLOCK), F32)
    lower_d, inv_d = eliminate(dot_high(sketch_d, jnp.concatenate([sketch_d, pad], axis=0), NT))
    basis_d[...] = dot_high(lower_d, sketch_d, NN)

    received(12, sfg_sib)
    reduce_first(13, sfg[c] + sfg_sib[...], packed, msg_g, z1_g, x1_g)

    @pl.when(z < OWNERS)
    def _():
        received(11, rs_d.at[pl.ds(0, Z - 1)])
        own_d[...] = dot_high(lower_d, total(rs_d, Z), NN) * (inv_d * (1.0 / 16.0))

    gather(18, own_d, coeff_d)

    gram_packed = reduce_second(13, z1_g, x1_g, mid_g, z2_g, x2_g)
    lane = lax.broadcasted_iota(jnp.int32, (8, LANES), 1)
    gram_g = jnp.concatenate(
        [jnp.where(lane < RANK, gram_packed if i == 0 else pltpu.roll(gram_packed, LANES - RANK * i, 1), 0.0) for i in range(4)],
        axis=0,
    )
    lower_g, inv_g = eliminate(gram_g)
    for i in range(2 * OWNERS):
        basis_g[i] = dot_high(lower_g, sg[i], NN)

    gathered(18, coeff_d)
    send(19, coeff_d.at[pl.ds(mine, OWNERS)], coeff_d.at[pl.ds(mine, OWNERS)], sibling)

    reduce_third(13, z2_g, x2_g, full_g)
    received(17, full_g.at[1 - c])
    coeff_g[...] = dot_high(lower_g, jnp.concatenate([full_g[0], full_g[1]], axis=1), NN) * (inv_g * (1.0 / 16.0))
    received(19, coeff_d.at[pl.ds(other, OWNERS)])

    sent(0, sd_sib)
    sent(1, sg_sib)
    sent(9, sfd_sib)
    sent(12, sfg_sib)
    sent(10, sg_sib)
    sent(19, sg_sib)
    for base, msg, z1, x1, z2, x2, full in (
        (2, msg_d, z1_d, x1_d, z2_d, x2_d, sd),
        (13, msg_g, z1_g, x1_g, z2_g, x2_g, full_g),
    ):
        sent(base, z1.at[pl.ds(0, Z - 1)])
        sent(base + 1, x1.at[pl.ds(0, XY - 1)])
        sent(base + 2, z2.at[pl.ds(0, Z - 1)])
        sent(base + 3, x2.at[pl.ds(0, XY - 1)])
        sent(base + 4, full.at[0])
    for scatter_stage, gather_stage, rs in ((7, 8, rs_g), (11, 18, rs_d)):
        @pl.when(z < OWNERS)
        def _():
            sent(scatter_stage, rs.at[pl.ds(0, OWNERS - 1)])
            sent(gather_stage, rs.at[pl.ds(0, Z - 1)])

        @pl.when(z == OWNERS)
        def _():
            sent(scatter_stage, rs.at[pl.ds(0, OWNERS)])


def finish_kernel(gg, eg, gd, ed, basis_g, coeff_g, basis_d, coeff_d, ug, ng, ud, nd):
    left = jnp.concatenate([basis_g[0], basis_g[1]], axis=1)
    update = dot_high(left, coeff_g[...], TN)
    ug[...] = update
    ng[...] = (gg[...].astype(F32) + eg[...]) - update
    right = jnp.concatenate([coeff_d[0], coeff_d[1]], axis=1)
    update = dot_high(basis_d[...], right, TN)
    ud[...] = update
    nd[...] = (gd[...].astype(F32) + ed[...]) - update


def local(grad_gate, error_gate, query_gate, grad_down, error_down, query_down):
    gg, eg, gd, ed = grad_gate[0], error_gate[0], grad_down[0], error_down[0]
    ff, rows = gg.shape
    tiles = ff // LANES
    vmem = pltpu.VMEM
    tile = (RANK, LANES)

    def stack(n, r=RANK):
        return vmem((n, r, LANES), F32)

    def reduce_buffers(extra):
        return [vmem((RANK + extra, LANES), F32), stack(Z, 16), stack(XY, 16 + extra), vmem(tile, F32), stack(Z, 16), stack(XY, 16), stack(2)]

    scratch = (
        [vmem((ff, rows), BF16), vmem((ff, rows), F32), vmem((RANK, rows), F32)]
        + [vmem((rows, ff), BF16), vmem((rows, ff), F32), vmem((RANK, ff), F32)]
        + [vmem((3, ff, rows), BF16), vmem((3, rows, ff), BF16)]
        + [stack(tiles), stack(OWNERS), stack(OWNERS), stack(Z), stack(tiles)]
        + [stack(2), vmem(tile, F32)] + reduce_buffers(8)
        + [stack(2), vmem(tile, F32)] + reduce_buffers(0)
        + [stack(tiles), stack(OWNERS), stack(OWNERS), stack(Z), vmem(tile, F32), vmem(tile, F32)]
        + [pltpu.SemaphoreType.DMA((6,)), pltpu.SemaphoreType.DMA((20,)), pltpu.SemaphoreType.DMA((20,))]
    )
    whole = pl.BlockSpec(memory_space=pltpu.VMEM)
    basis_g, coeff_g, basis_d, coeff_d = pl.pallas_call(
        exchange_kernel,
        out_shape=[
            jax.ShapeDtypeStruct((tiles, RANK, LANES), F32),
            jax.ShapeDtypeStruct((RANK, rows), F32),
            jax.ShapeDtypeStruct((RANK, rows), F32),
            jax.ShapeDtypeStruct((tiles, RANK, LANES), F32),
        ],
        in_specs=[pl.BlockSpec(memory_space=pl.ANY)] * 6,
        out_specs=[whole] * 4,
        scratch_shapes=scratch,
        compiler_params=pltpu.CompilerParams(collective_id=0, has_side_effects=True, vmem_limit_bytes=48 * 2**20),
    )(gg, eg, query_gate, gd, ed, query_down)

    gate = pl.BlockSpec((BLOCK, rows), lambda i: (i, 0))
    down = pl.BlockSpec((rows, BLOCK), lambda i: (0, i))
    small = pl.BlockSpec((RANK, rows), lambda i: (0, 0))
    pair = pl.BlockSpec((2, RANK, LANES), lambda i: (i, 0, 0))
    gate_shape = jax.ShapeDtypeStruct((ff, rows), F32)
    down_shape = jax.ShapeDtypeStruct((rows, ff), F32)
    ug, ng, ud, nd = pl.pallas_call(
        finish_kernel,
        grid=(ff // BLOCK,),
        out_shape=[gate_shape, gate_shape, down_shape, down_shape],
        in_specs=[gate, gate, down, down, pair, small, small, pair],
        out_specs=[gate, gate, down, down],
        compiler_params=pltpu.CompilerParams(vmem_limit_bytes=48 * 2**20),
    )(gg, eg, gd, ed, basis_g, coeff_g, basis_d, coeff_d)
    return ug, ng[None], ud, nd[None]


def solution(mesh):
    in_specs = (
        P("dp", "tensor", None),
        P("dp", "tensor", None),
        P(),
        P("dp", None, "tensor"),
        P("dp", None, "tensor"),
        P(None, "tensor"),
    )
    out_specs = (
        P("tensor", None),
        P("dp", "tensor", None),
        P(None, "tensor"),
        P("dp", None, "tensor"),
    )
    return jax.shard_map(local, mesh=mesh, in_specs=in_specs, out_specs=out_specs, check_vma=False)
```

time: 570 us -> 58.6 us (0.10)
  waiting for transfers between devices: 452 us -> 0 us
  blocking collectives: 60.5 us -> 0 us
  Pallas kernels: 0 us -> 52.1 us
  matrix products: 22.8 us -> 0 us
  other arithmetic: 18.3 us -> 0 us
  between operations: 13.9 us -> 0.66 us
    psum x3 -> x0, waiting for transfers between devices: 452 us -> none  [the longest x1 246 us: local(): coeff_gate = lax.psum(local_gate, ('dp', 'tensor')) / workers]
    psum x1 -> x0, blocking collectives: 60.5 us -> none  [local(): gram = lax.psum(contract_last(sketch_gate, sketch_gate), 'tensor')]
    pallas_call x0 -> x2, Pallas kernels: none -> 52.1 us  [the longest x1 45.7 us: local(): pl.pallas_call(exchange_kernel, out_shape=[jax.ShapeDtypeStruct((tiles, R...]
    dot_general x8 -> x0, matrix products: 20.5 us -> none  [the longest x4 10.9 us: contract_last(): lax.dot_general(left, right, (((1,), (1,)), ((), ())), precision=HIGH)]
    another operation x10 -> x0, other arithmetic: 13.4 us -> none  [the longest x6 7.19 us: cholesky_rows(): lower = jnp.linalg.cholesky(gram)]
  transfers between devices with their start and end apart: 3 -> 0, of which waited for: 3 -> 0; matrix products, arithmetic and copies ran while one was open for 1% -> 0% of each run, Pallas kernels for 0% -> 0%
where the time goes in v1:
time: 58.6 us; the launch traced here: 58.3 us
  Pallas kernels  52.1 us (89%)
  local copies, waits for them, and re-layouts  5.55 us (9%)
  between operations  0.66 us (1%)
    pallas_call x1, Pallas kernels, local(): pl.pallas_call(exchange_kernel, out_shape=[jax.ShapeDtypeStruct((tiles, R...  45.7 us
    pallas_call x1, Pallas kernels, local(): pl.pallas_call(finish_kernel, grid=(ff // BLOCK,), out_shape=[gate_shape,...  6.44 us
    unnamed x12, local copies, waits for them, and re-layouts  5.55 us

profile of v1, /device:TPU:1, one launch (start us, length us, event | category | flops | bytes accessed | tf_op | source)
XLA Modules:
  0.0 58.3 jit_solution(12106469943859005179)
XLA Ops:
  0.6 0.0 copy-start
  0.6 1.5 %copy-done = f32[1,1792,256]{2,1,0:T(8,128)S(1)} copy-done((f32[1,1792,256]{2,1,0:T(8,128)S(1)}, f32[1,1792,256]{2,1,0:T(8,128)}, u32[]{:S(2)}) %copy-start) | copy-done | bytes 1835032
  2.1 0.0 copy-start.2
  2.1 1.2 %copy-done.2 = bf16[1,1792,256]{2,1,0:T(8,128)(2,1)S(1)} copy-done((bf16[1,1792,256]{2,1,0:T(8,128)(2,1)S(1)}, bf16[1,1792,256]{2,1,0:T(8,128)(2,1)}, u32[]{:S(2)}) %copy-start.2) | copy-done | bytes 917528
  3.3 0.0 copy-start.3
  3.3 1.2 %copy-done.3 = bf16[1,256,1792]{2,1,0:T(8,128)(2,1)S(1)} copy-done((bf16[1,256,1792]{2,1,0:T(8,128)(2,1)S(1)}, bf16[1,256,1792]{2,1,0:T(8,128)(2,1)}, u32[]{:S(2)}) %copy-start.3) | copy-done | bytes 917528
  4.5 0.0 copy-start.4
  4.5 0.9 %copy-done.4 = f32[32,1792]{1,0:T(8,128)S(1)} copy-done((f32[32,1792]{1,0:T(8,128)S(1)}, f32[32,1792]{1,0:T(8,128)}, u32[]{:S(2)}) %copy-start.4) | copy-done | bytes 229400
  5.4 0.0 copy-start.5
  5.4 0.8 %copy-done.5 = f32[32,256]{1,0:T(8,128)S(1)} copy-done((f32[32,256]{1,0:T(8,128)S(1)}, f32[32,256]{1,0:T(8,128)}, u32[]{:S(2)}) %copy-start.5) | copy-done | bytes 32792
  6.2 0.0 copy-start.1
  6.2 45.7 %shard_map.93 = (f32[14,32,128]{2,1,0:T(8,128)S(1)}, f32[32,256]{1,0:T(8,128)S(1)}, f32[32,256]{1,0:T(8,128)S(1)}, f32[14,32,128]{2,1,0:T(8,128)S(1)}) custom-call(bf16[1792,256]{1,0:T(8,128)(2,1)S(1)} %bitcast.10, f32[1792,256]{1,0:T(8,128)S(1)} %bitcast.6, f32[32,256]{1,0:T(8,128)S(1)} %copy-done.5, bf16[256,1792]{1,0:T(8,128)(2,1)S(1)} %bitcast.12, ...), custom_call_target="tpu_custom_call" | custom-call | tf_op jit(solution)/shard_map/pallas_call | solution.py:357
  51.9 0.0 copy-done.1
  51.9 6.4 %shard_map.94 = (f32[1792,256]{1,0:T(8,128)}, f32[1792,256]{1,0:T(8,128)}, f32[256,1792]{1,0:T(8,128)}, f32[256,1792]{1,0:T(8,128)}) custom-call(bf16[1792,256]{1,0:T(8,128)(2,1)S(1)} %bitcast.11, f32[1792,256]{1,0:T(8,128)S(1)} %bitcast.7, bf16[256,1792]{1,0:T(8,128)(2,1)S(1)} %bitcast.13, f32[256,1792]{1,0:T(8,128)S(1)} %bitcast.9, ...), custom_call_target="tpu_custom_call" | custom-call | tf_op jit(solution)/shard_map/pallas_call | solution.py:377
Async XLA Ops:
  0.6 1.5 %copy-start = (f32[1,1792,256]{2,1,0:T(8,128)S(1)}, f32[1,1792,256]{2,1,0:T(8,128)}, u32[]{:S(2)}) copy-start(f32[1,1792,256]{2,1,0:T(8,128)} %param.7) | copy-start | bytes 5505028
  2.1 1.2 %copy-start.2 = (bf16[1,1792,256]{2,1,0:T(8,128)(2,1)S(1)}, bf16[1,1792,256]{2,1,0:T(8,128)(2,1)}, u32[]{:S(2)}) copy-start(bf16[1,1792,256]{2,1,0:T(8,128)(2,1)} %param.6) | copy-start | bytes 2752516
  3.3 1.2 %copy-start.3 = (bf16[1,256,1792]{2,1,0:T(8,128)(2,1)S(1)}, bf16[1,256,1792]{2,1,0:T(8,128)(2,1)}, u32[]{:S(2)}) copy-start(bf16[1,256,1792]{2,1,0:T(8,128)(2,1)} %param.9) | copy-start | bytes 2752516
  4.5 0.9 %copy-start.4 = (f32[32,1792]{1,0:T(8,128)S(1)}, f32[32,1792]{1,0:T(8,128)}, u32[]{:S(2)}) copy-start(f32[32,1792]{1,0:T(8,128)} %qd_hbm.1) | copy-start | bytes 688132
  5.4 0.8 %copy-start.5 = (f32[32,256]{1,0:T(8,128)S(1)}, f32[32,256]{1,0:T(8,128)}, u32[]{:S(2)}) copy-start(f32[32,256]{1,0:T(8,128)} %qg_hbm.1) | copy-start | bytes 98308
  6.2 45.7 %copy-start.1 = (f32[1,256,1792]{2,1,0:T(8,128)S(1)}, f32[1,256,1792]{2,1,0:T(8,128)}, u32[]{:S(2)}) copy-start(f32[1,256,1792]{2,1,0:T(8,128)} %param.10) | copy-start | bytes 5505028

commit v2 on v1

--- a/solution.py
+++ b/solution.py
@@ -75,14 +75,24 @@
     return a[:, RANK : 2 * RANK], inverse
 
 
+def left_six(x):
+    hi, mid, lo = split3(x)
+    return jnp.concatenate([hi, hi, mid, hi, lo, mid], axis=0)
+
+
+def right_six(x):
+    hi, mid, lo = split3(x)
+    return jnp.concatenate([hi, mid, hi, lo, hi, mid], axis=0)
+
+
 def exchange_kernel(
     gg_hbm, eg_hbm, qg_hbm, gd_hbm, ed_hbm, qd_hbm,
-    basis_g, coeff_g, basis_d, coeff_d,
-    gg, eg, qg, gd, ed, qd, fg, fd,
+    full_g, full_d, left_g, right_g, left_d, coeff_d,
+    gg, eg, qg, gd, ed, qd, mg_in, md_in, mg, md,
     sg_part, sg_sib, sg_half, rs_g, sg,
-    sfg, sfg_sib, msg_g, z1_g, x1_g, mid_g, z2_g, x2_g, full_g,
+    sfg, sfg_sib, msg_g, z1_g, x1_g, mid_g, z2_g, x2_g, sum_g,
     sd_part, sd_sib, msg_d, z1_d, x1_d, mid_d, z2_d, x2_d, sd,
-    sfd, sfd_sib, sfd_half, rs_d, own_g, own_d,
+    sfd, sfd_sib, sfd_half, rs_d, own_g, own_d, co_d,
     load_sem, send_sem, recv_sem,
 ):
     dp, t = lax.axis_index("dp"), lax.axis_index("tensor")
@@ -118,15 +128,15 @@
         pltpu.make_async_copy(ref, ref, send_sem.at[stage]).wait()
 
     blocks = gg.shape[0] // BLOCK
+    g_half, d_half = mg_in.shape[0], md_in.shape[0]
     for load in loads[:3]:
         load.wait()
     sd_sum = None
     for b in range(blocks):
         cols = pl.ds(b * BLOCK, BLOCK)
-        parts = split3(gd[:, cols].astype(F32) + ed[:, cols])
-        for i in range(3):
-            fd[i, :, cols] = parts[i]
-        term = dot6(rows3(qd[:, cols]), parts, NT)
+        block = gd[:, cols].astype(F32) + ed[:, cols]
+        full_d[:, cols] = block
+        term = dot6(rows3(qd[:, cols]), split3(block), NT)
         sd_sum = term if sd_sum is None else sd_sum + term
     sd_part[0] = sd_sum[:, :LANES]
     sd_part[1] = sd_sum[:, LANES:]
@@ -135,10 +145,9 @@
     qg3 = rows3(qg[...])
     for b in range(blocks):
         rows = pl.ds(b * BLOCK, BLOCK)
-        parts = split3(gg[rows, :].astype(F32) + eg[rows, :])
-        for i in range(3):
-            fg[i, rows, :] = parts[i]
-        term = dot6(qg3, parts, NT)
+        block = gg[rows, :].astype(F32) + eg[rows, :]
+        full_g[rows, :] = block
+        term = dot6(qg3, split3(block), NT)
         sg_part[2 * b] = term[:, :LANES]
         sg_part[2 * b + 1] = term[:, LANES:]
 
@@ -147,11 +156,11 @@
     mine, other = OWNERS * c, OWNERS * (1 - c)
     send(0, sd_part.at[1 - c], sd_sib, sibling)
     send(1, sg_part.at[pl.ds(other, OWNERS)], sg_sib, sibling)
-
-    def reduce_first(base, value, extra, msg, z1, x1):
-        msg[0:32] = value
-        if extra is not None:
-            msg[32:40] = extra
+    send(20, full_d.at[pl.ds(pl.multiple_of((1 - c) * d_half, LANES), d_half)], md_in, sibling)
+    send(21, full_g.at[pl.ds(pl.multiple_of((1 - c) * g_half, LANES), g_half)], mg_in, sibling)
+
+    def reduce_first(base, value, msg, z1, x1):
+        msg[...] = value
         z1[z] = msg[0:16]
         high = msg.at[pl.ds(16, msg.shape[0] - 16)]
         x1[t] = high[...]
@@ -209,12 +218,26 @@
             received(stage, dst.at[pl.ds(0, OWNERS)])
 
     received(0, sd_sib)
-    reduce_first(2, sd_part[c] + sd_sib[...], None, msg_d, z1_d, x1_d)
+    reduce_first(2, sd_part[c] + sd_sib[...], msg_d, z1_d, x1_d)
     received(1, sg_sib)
     for i in range(OWNERS):
         sg_half[i] = sg_part[mine + i] + sg_sib[i]
     scatter(7, sg_half, rs_g)
 
+    received(20, md_in)
+    for b in range(blocks):
+        cols = pl.ds(b * BLOCK, BLOCK)
+        block = full_d[pl.ds(pl.multiple_of(c * d_half, LANES), d_half), cols] + md_in[:, cols]
+        hi, mid, lo = split3(block)
+        md[0:d_half, cols] = hi
+        md[d_half : 2 * d_half, cols] = mid
+        md[2 * d_half :, cols] = lo
+    received(21, mg_in)
+    for b in range(OWNERS):
+        parts = split3(full_g[pl.ds(pl.multiple_of(c * g_half + b * LANES, LANES), LANES), :] + mg_in[pl.ds(b * LANES, LANES), :])
+        for i in range(3):
+            mg[i, pl.ds(b * LANES, LANES), :] = parts[i]
+
     reduce_second(2, z1_d, x1_d, mid_d, z2_d, x2_d)
 
     @pl.when(z < OWNERS)
@@ -225,55 +248,66 @@
     gather(8, own_g, sg)
 
     reduce_third(2, z2_d, x2_d, sd)
-    received(6, sd.at[1 - c])
-
-    sketch_d = jnp.concatenate([sd[0], sd[1]], axis=1)
-    sd3 = rows3(sketch_d)
+
+    hi, mid, lo = split3(sd[c])
+    stacked = jnp.concatenate(
+        [
+            jnp.concatenate([hi, hi], axis=1),
+            jnp.concatenate([mid, mid], axis=1),
+            jnp.concatenate([lo, jnp.zeros_like(lo)], axis=1),
+        ],
+        axis=0,
+    )
     for b in range(blocks):
         cols = pl.ds(b * BLOCK, BLOCK)
-        term = dot6(sd3, [fd[i, :, cols] for i in range(3)], NN)
+        a = dot(stacked, md[0 : 2 * d_half, cols], NN)
+        small = dot(hi, md[2 * d_half :, cols], NN) + a[2 * RANK :]
+        term = a[:RANK] + (a[RANK : 2 * RANK] + small)
         sfd[2 * b] = term[:, :LANES]
         sfd[2 * b + 1] = term[:, LANES:]
     send(9, sfd.at[pl.ds(other, OWNERS)], sfd_sib, sibling)
 
     gathered(8, sg)
     send(10, sg.at[pl.ds(mine, OWNERS)], sg.at[pl.ds(mine, OWNERS)], sibling)
+    sfg_sum = None
+    gram_sum = None
+    for b in range(0, OWNERS, 2):
+        n = min(2, OWNERS - b)
+        rows = pl.ds(b * LANES, n * LANES)
+        tile = jnp.concatenate([sg[mine + b + i] for i in range(n)], axis=1)
+        term = dot6(rows3(tile), [mg[i, rows, :] for i in range(3)], NN)
+        sfg_sum = term if sfg_sum is None else sfg_sum + term
+        pad = jnp.zeros((LANES - RANK, n * LANES), F32)
+        term = dot_high(tile, jnp.concatenate([tile, pad], axis=0), NT)
+        gram_sum = term if gram_sum is None else gram_sum + term
+    packed = gram_sum[0:8]
+    for i in range(1, 4):
+        packed = packed + pltpu.roll(gram_sum[8 * i : 8 * i + 8], RANK * i, 1)
+    for i in range(2):
+        sfg[i, 0:RANK] = sfg_sum[:, i * LANES : (i + 1) * LANES]
+        sfg[i, RANK:] = packed
+    send(12, sfg.at[1 - c], sfg_sib, sibling)
+
     received(9, sfd_sib)
     for i in range(OWNERS):
         sfd_half[i] = sfd[mine + i] + sfd_sib[i]
     scatter(11, sfd_half, rs_d)
 
-    received(10, sg.at[pl.ds(other, OWNERS)])
-    sfg_sum = None
-    gram_sum = None
-    zeros = jnp.zeros((LANES - RANK, BLOCK), F32)
-    for b in range(blocks):
-        rows = pl.ds(b * BLOCK, BLOCK)
-        tile = jnp.concatenate([sg[2 * b], sg[2 * b + 1]], axis=1)
-        term = dot6(rows3(tile), [fg[i, rows, :] for i in range(3)], NN)
-        sfg_sum = term if sfg_sum is None else sfg_sum + term
-        term = dot_high(tile, jnp.concatenate([tile, zeros], axis=0), NT)
-        gram_sum = term if gram_sum is None else gram_sum + term
-    packed = gram_sum[0:8]
-    for i in range(1, 4):
-        packed = packed + pltpu.roll(gram_sum[8 * i : 8 * i + 8], RANK * i, 1)
-    sfg[0] = sfg_sum[:, :LANES]
-    sfg[1] = sfg_sum[:, LANES:]
-    send(12, sfg.at[1 - c], sfg_sib, sibling)
-
+    received(12, sfg_sib)
+    reduce_first(13, sfg[c] + sfg_sib[...], msg_g, z1_g, x1_g)
+
+    received(6, sd.at[1 - c])
+    sketch_d = jnp.concatenate([sd[0], sd[1]], axis=1)
     pad = jnp.zeros((LANES - RANK, BLOCK), F32)
     lower_d, inv_d = eliminate(dot_high(sketch_d, jnp.concatenate([sketch_d, pad], axis=0), NT))
-    basis_d[...] = dot_high(lower_d, sketch_d, NN)
-
-    received(12, sfg_sib)
-    reduce_first(13, sfg[c] + sfg_sib[...], packed, msg_g, z1_g, x1_g)
 
     @pl.when(z < OWNERS)
     def _():
         received(11, rs_d.at[pl.ds(0, Z - 1)])
         own_d[...] = dot_high(lower_d, total(rs_d, Z), NN) * (inv_d * (1.0 / 16.0))
 
-    gather(18, own_d, coeff_d)
+    gather(18, own_d, co_d)
+    left_d[...] = jnp.transpose(left_six(dot_high(lower_d, sketch_d, NN)))
 
     gram_packed = reduce_second(13, z1_g, x1_g, mid_g, z2_g, x2_g)
     lane = lax.broadcasted_iota(jnp.int32, (8, LANES), 1)
@@ -282,26 +316,31 @@
         axis=0,
     )
     lower_g, inv_g = eliminate(gram_g)
+    received(10, sg.at[pl.ds(other, OWNERS)])
     for i in range(2 * OWNERS):
-        basis_g[i] = dot_high(lower_g, sg[i], NN)
-
-    gathered(18, coeff_d)
-    send(19, coeff_d.at[pl.ds(mine, OWNERS)], coeff_d.at[pl.ds(mine, OWNERS)], sibling)
-
-    reduce_third(13, z2_g, x2_g, full_g)
-    received(17, full_g.at[1 - c])
-    coeff_g[...] = dot_high(lower_g, jnp.concatenate([full_g[0], full_g[1]], axis=1), NN) * (inv_g * (1.0 / 16.0))
-    received(19, coeff_d.at[pl.ds(other, OWNERS)])
+        left_g[pl.ds(i * LANES, LANES), :] = jnp.transpose(left_six(dot_high(lower_g, sg[i], NN)))
+
+    gathered(18, co_d)
+    send(19, co_d.at[pl.ds(mine, OWNERS)], co_d.at[pl.ds(mine, OWNERS)], sibling)
+
+    reduce_third(13, z2_g, x2_g, sum_g)
+    received(17, sum_g.at[1 - c])
+    coeff = dot_high(lower_g, jnp.concatenate([sum_g[0], sum_g[1]], axis=1), NN) * (inv_g * (1.0 / 16.0))
+    right_g[...] = right_six(coeff)
+    received(19, co_d.at[pl.ds(other, OWNERS)])
+    coeff_d[...] = co_d[...]
 
     sent(0, sd_sib)
     sent(1, sg_sib)
+    sent(20, md_in)
+    sent(21, mg_in)
     sent(9, sfd_sib)
     sent(12, sfg_sib)
     sent(10, sg_sib)
     sent(19, sg_sib)
-    for base, msg, z1, x1, z2, x2, full in (
-        (2, msg_d, z1_d, x1_d, z2_d, x2_d, sd),
-        (13, msg_g, z1_g, x1_g, z2_g, x2_g, full_g),
+    for base, z1, x1, z2, x2, full in (
+        (2, z1_d, x1_d, z2_d, x2_d, sd),
+        (13, z1_g, x1_g, z2_g, x2_g, sum_g),
     ):
         sent(base, z1.at[pl.ds(0, Z - 1)])
         sent(base + 1, x1.at[pl.ds(0, XY - 1)])
@@ -319,15 +358,29 @@
             sent(scatter_stage, rs.at[pl.ds(0, OWNERS)])
 
 
-def finish_kernel(gg, eg, gd, ed, basis_g, coeff_g, basis_d, coeff_d, ug, ng, ud, nd):
-    left = jnp.concatenate([basis_g[0], basis_g[1]], axis=1)
-    update = dot_high(left, coeff_g[...], TN)
-    ug[...] = update
-    ng[...] = (gg[...].astype(F32) + eg[...]) - update
-    right = jnp.concatenate([coeff_d[0], coeff_d[1]], axis=1)
-    update = dot_high(basis_d[...], right, TN)
-    ud[...] = update
-    nd[...] = (gd[...].astype(F32) + ed[...]) - update
+def finish_kernel(full_g, full_d, left_g, right_g, left_d, coeff_d, ug_hbm, ng_hbm, ud_hbm, nd_hbm, ug, ng, ud, nd, sem):
+    copies = []
+
+    def store(src, dst):
+        copies.append(pltpu.make_async_copy(src, dst, sem.at[len(copies)]))
+        copies[-1].start()
+
+    for b in range(full_g.shape[0] // BLOCK):
+        part = (pl.ds(b * BLOCK, BLOCK), slice(None))
+        update = dot(left_g[part], right_g[...], NN)
+        ug[part] = update
+        ng[part] = full_g[part] - update
+        store(ug.at[part], ug_hbm.at[part])
+        store(ng.at[part], ng_hbm.at[part])
+        part = (slice(None), pl.ds(b * BLOCK, BLOCK))
+        right = right_six(jnp.concatenate([coeff_d[2 * b], coeff_d[2 * b + 1]], axis=1))
+        update = dot(left_d[...], right, NN)
+        ud[part] = update
+        nd[part] = full_d[part] - update
+        store(ud.at[part], ud_hbm.at[part])
+        store(nd.at[part], nd_hbm.at[part])
+    for copy in copies:
+        copy.wait()
 
 
 def local(grad_gate, error_gate, query_gate, grad_down, error_down, query_down):
@@ -346,42 +399,38 @@
     scratch = (
         [vmem((ff, rows), BF16), vmem((ff, rows), F32), vmem((RANK, rows), F32)]
         + [vmem((rows, ff), BF16), vmem((rows, ff), F32), vmem((RANK, ff), F32)]
-        + [vmem((3, ff, rows), BF16), vmem((3, rows, ff), BF16)]
+        + [vmem((ff // 2, rows), F32), vmem((rows // 2, ff), F32), vmem((3, ff // 2, rows), BF16), vmem((3 * rows // 2, ff), BF16)]
         + [stack(tiles), stack(OWNERS), stack(OWNERS), stack(Z), stack(tiles)]
-        + [stack(2), vmem(tile, F32)] + reduce_buffers(8)
+        + [stack(2, RANK + 8), vmem((RANK + 8, LANES), F32)] + reduce_buffers(8)
         + [stack(2), vmem(tile, F32)] + reduce_buffers(0)
-        + [stack(tiles), stack(OWNERS), stack(OWNERS), stack(Z), vmem(tile, F32), vmem(tile, F32)]
-        + [pltpu.SemaphoreType.DMA((6,)), pltpu.SemaphoreType.DMA((20,)), pltpu.SemaphoreType.DMA((20,))]
+        + [stack(tiles), stack(OWNERS), stack(OWNERS), stack(Z), vmem(tile, F32), vmem(tile, F32), stack(tiles)]
+        + [pltpu.SemaphoreType.DMA((6,)), pltpu.SemaphoreType.DMA((22,)), pltpu.SemaphoreType.DMA((22,))]
     )
     whole = pl.BlockSpec(memory_space=pltpu.VMEM)
-    basis_g, coeff_g, basis_d, coeff_d = pl.pallas_call(
+    gate_shape, down_shape = (ff, rows), (rows, ff)
+    shapes = [
+        (gate_shape, F32), (down_shape, F32), ((ff, 6 * RANK), BF16), ((6 * RANK, rows), BF16),
+        ((rows, 6 * RANK), BF16), ((tiles, RANK, LANES), F32),
+    ]
+    inputs = [pltpu.with_memory_space_constraint(a, pltpu.HBM) for a in (gg, eg, query_gate, gd, ed, query_down)]
+    middle = pl.pallas_call(
         exchange_kernel,
-        out_shape=[
-            jax.ShapeDtypeStruct((tiles, RANK, LANES), F32),
-            jax.ShapeDtypeStruct((RANK, rows), F32),
-            jax.ShapeDtypeStruct((RANK, rows), F32),
-            jax.ShapeDtypeStruct((tiles, RANK, LANES), F32),
-        ],
-        in_specs=[pl.BlockSpec(memory_space=pl.ANY)] * 6,
-        out_specs=[whole] * 4,
+        out_shape=[pltpu.VMEM(shape, dtype) for shape, dtype in shapes],
+        in_specs=[pl.BlockSpec(memory_space=pltpu.HBM)] * 6,
+        out_specs=[whole] * len(shapes),
         scratch_shapes=scratch,
-        compiler_params=pltpu.CompilerParams(collective_id=0, has_side_effects=True, vmem_limit_bytes=48 * 2**20),
-    )(gg, eg, query_gate, gd, ed, query_down)
-
-    gate = pl.BlockSpec((BLOCK, rows), lambda i: (i, 0))
-    down = pl.BlockSpec((rows, BLOCK), lambda i: (0, i))
-    small = pl.BlockSpec((RANK, rows), lambda i: (0, 0))
-    pair = pl.BlockSpec((2, RANK, LANES), lambda i: (i, 0, 0))
-    gate_shape = jax.ShapeDtypeStruct((ff, rows), F32)
-    down_shape = jax.ShapeDtypeStruct((rows, ff), F32)
+        compiler_params=pltpu.CompilerParams(collective_id=0, has_side_effects=True, vmem_limit_bytes=32 * 2**20),
+    )(*inputs)
+
+    outs = [gate_shape, gate_shape, down_shape, down_shape]
     ug, ng, ud, nd = pl.pallas_call(
         finish_kernel,
-        grid=(ff // BLOCK,),
-        out_shape=[gate_shape, gate_shape, down_shape, down_shape],
-        in_specs=[gate, gate, down, down, pair, small, small, pair],
-        out_specs=[gate, gate, down, down],
-        compiler_params=pltpu.CompilerParams(vmem_limit_bytes=48 * 2**20),
-    )(gg, eg, gd, ed, basis_g, coeff_g, basis_d, coeff_d)
+        out_shape=[jax.ShapeDtypeStruct(shape, F32) for shape in outs],
+        in_specs=[whole] * len(shapes),
+        out_specs=[pl.BlockSpec(memory_space=pl.ANY)] * 4,
+        scratch_shapes=[vmem(shape, F32) for shape in outs] + [pltpu.SemaphoreType.DMA((4 * (ff // BLOCK),))],
+        compiler_params=pltpu.CompilerParams(vmem_limit_bytes=32 * 2**20),
+    )(*middle)
     return ug, ng[None], ud, nd[None]
 
 

time: 58.6 us -> 46.7 us (0.80)
  Pallas kernels: 52.1 us -> 45.9 us
  local copies, waits for them, and re-layouts: 5.55 us -> 0 us
    pallas_call x2, Pallas kernels: 52.1 us -> 45.9 us  [the longest x1 42.5 us: local(): pl.pallas_call(exchange_kernel, out_shape=[pltpu.VMEM(shape, dtype) for s...]
    unnamed x12 -> x0, local copies, waits for them, and re-layouts: 5.55 us -> none
where the time goes in v2:
time: 46.7 us; the launch traced here: 46.6 us
  Pallas kernels  45.9 us (98%)
  between operations  0.64 us (1%)
    pallas_call x1, Pallas kernels, local(): pl.pallas_call(exchange_kernel, out_shape=[pltpu.VMEM(shape, dtype) for s...  42.5 us
    pallas_call x1, Pallas kernels, local(): pl.pallas_call(finish_kernel, out_shape=[jax.ShapeDtypeStruct(shape, F32)...  3.41 us

profile of v2, /device:TPU:1, one launch (start us, length us, event | category | flops | bytes accessed | tf_op | source)
XLA Modules:
  0.0 46.6 jit_solution(15850695115426728927)
XLA Ops:
  0.6 42.5 %shard_map.93 = (f32[1792,256]{1,0:T(8,128)S(1)}, f32[256,1792]{1,0:T(8,128)S(1)}, bf16[1792,192]{1,0:T(8,128)(2,1)S(1)}, bf16[192,256]{1,0:T(8,128)(2,1)S(1)}, ...) custom-call(bf16[1792,256]{1,0:T(8,128)(2,1)} %bitcast.8, f32[1792,256]{1,0:T(8,128)} %bitcast.6, ...), custom_call_target="tpu_custom_call" | custom-call | tf_op jit(solution)/shard_map/pallas_call | solution.py:416
  43.2 3.4 %shard_map.94 = (f32[1792,256]{1,0:T(8,128)}, f32[1792,256]{1,0:T(8,128)}, f32[256,1792]{1,0:T(8,128)}, f32[256,1792]{1,0:T(8,128)}) custom-call(f32[1792,256]{1,0:T(8,128)S(1)} %get-tuple-element.14.full_g, f32[256,1792]{1,0:T(8,128)S(1)} %get-tuple-element.15.full_d, bf16[1792,192]{1,0:T(8,128)(2,1)S(1)} %get-tuple-element.16.left_g, ...), custom_call_target="tpu_custom_call" | custom-call | tf_op jit(solution)/shard_map/pallas_call | solution.py:426

commit v3 on v2

--- a/solution.py
+++ b/solution.py
@@ -9,7 +9,6 @@
 
 MESH = pl.DeviceIdType.MESH
 F32, BF16 = jnp.float32, jnp.bfloat16
-HIGH = lax.Precision.HIGHEST
 NN = (((1,), (0,)), ((), ()))
 NT = (((1,), (1,)), ((), ()))
 TN = (((0,), (0,)), ((), ()))
@@ -17,7 +16,9 @@
 BLOCK = 256
 RANK = 32
 Z, XY = 8, 16
-OWNERS = 7
+HALF = 7
+CHUNK = 4
+SPREAD = 16
 Z_ORDER = (4, 3, 5, 2, 6, 1, 7)
 XY_ORDER = sorted(
     ((dx, dy) for dx in range(4) for dy in range(4) if dx or dy),
@@ -38,10 +39,6 @@
 
 def dot(a, b, dims):
     return lax.dot_general(a, b, dims, preferred_element_type=F32)
-
-
-def dot_high(a, b, dims):
-    return lax.dot_general(a, b, dims, precision=HIGH, preferred_element_type=F32)
 
 
 def dot6(left3, right, dims):
@@ -53,6 +50,16 @@
     return a[:RANK] + ((a[RANK : 2 * RANK] + b[:RANK]) + small)
 
 
+def tile_of(ref, half, i):
+    return jnp.concatenate([ref[half, k, CHUNK * i : CHUNK * (i + 1)] for k in range(Z)], axis=0)
+
+
+def put_tile(ref, j, tile):
+    i = CHUNK * (j % HALF)
+    for k in range(Z):
+        ref[j // HALF, k, i : i + CHUNK] = tile[k * CHUNK : (k + 1) * CHUNK]
+
+
 def total(ref, n):
     out = ref[0]
     for i in range(1, n):
@@ -64,20 +71,26 @@
     rows = lax.broadcasted_iota(jnp.int32, (RANK, LANES), 0)
     lanes = lax.broadcasted_iota(jnp.int32, (RANK, LANES), 1)
     a = gram + (lanes == rows + RANK).astype(F32)
-    index = lax.broadcasted_iota(jnp.int32, (RANK, 1), 0)
-    inverse = jnp.zeros((RANK, 1), F32)
-    for k in range(RANK):
-        row = a[k : k + 1, :]
-        inv = 1.0 / a[k : k + 1, k : k + 1]
-        inverse = jnp.where(index == k, inv, inverse)
-        column = a[:, k : k + 1]
-        a = a - jnp.where(index > k, column * inv, 0.0) * row
-    return a[:, RANK : 2 * RANK], inverse
+    for first in range(0, RANK, SPREAD):
+        columns = [jnp.broadcast_to(a[:, k : k + 1], (RANK, LANES)) for k in range(first, first + SPREAD)]
+        for i, column in enumerate(columns):
+            k = first + i
+            factor = jnp.where(rows > k, column, 0.0) * (1.0 / column[k : k + 1])
+            for later in range(i + 1, SPREAD):
+                columns[later] = columns[later] - factor * columns[later][k : k + 1]
+            a = a - factor * a[k : k + 1]
+    pivots = jnp.sum(jnp.where(lanes == rows, a, 0.0), axis=1, keepdims=True)
+    return a[:, RANK : 2 * RANK], jnp.transpose(a)[RANK : 2 * RANK], 1.0 / pivots
 
 
 def left_six(x):
     hi, mid, lo = split3(x)
     return jnp.concatenate([hi, hi, mid, hi, lo, mid], axis=0)
+
+
+def left_lanes(x):
+    hi, mid, lo = split3(x)
+    return jnp.concatenate([hi, hi, mid, hi, lo, mid], axis=1)
 
 
 def right_six(x):
@@ -90,7 +103,7 @@
     full_g, full_d, left_g, right_g, left_d, coeff_d,
     gg, eg, qg, gd, ed, qd, mg_in, md_in, mg, md,
     sg_part, sg_sib, sg_half, rs_g, sg,
-    sfg, sfg_sib, msg_g, z1_g, x1_g, mid_g, z2_g, x2_g, sum_g,
+    sfg, sfg_sib, gram_own, gram_sib, msg_g, z1_g, x1_g, mid_g, z2_g, x2_g, sum_g,
     sd_part, sd_sib, msg_d, z1_d, x1_d, mid_d, z2_d, x2_d, sd,
     sfd, sfd_sib, sfd_half, rs_d, own_g, own_d, co_d,
     load_sem, send_sem, recv_sem,
@@ -148,16 +161,13 @@
         block = gg[rows, :].astype(F32) + eg[rows, :]
         full_g[rows, :] = block
         term = dot6(qg3, split3(block), NT)
-        sg_part[2 * b] = term[:, :LANES]
-        sg_part[2 * b + 1] = term[:, LANES:]
+        put_tile(sg_part, 2 * b, term[:, :LANES])
+        put_tile(sg_part, 2 * b + 1, term[:, LANES:])
 
     pl.semaphore_wait(barrier, 1 + len(z_peers) + len(xy_peers))
 
-    mine, other = OWNERS * c, OWNERS * (1 - c)
+    send(1, sg_part.at[1 - c], sg_sib, sibling)
     send(0, sd_part.at[1 - c], sd_sib, sibling)
-    send(1, sg_part.at[pl.ds(other, OWNERS)], sg_sib, sibling)
-    send(20, full_d.at[pl.ds(pl.multiple_of((1 - c) * d_half, LANES), d_half)], md_in, sibling)
-    send(21, full_g.at[pl.ds(pl.multiple_of((1 - c) * g_half, LANES), g_half)], mg_in, sibling)
 
     def reduce_first(base, value, msg, z1, x1):
         msg[...] = value
@@ -191,38 +201,29 @@
         full[c, 16:32] = total(z2, Z)
         send(base + 4, full.at[c], full.at[c], sibling)
 
-    def scatter(stage, half, rs):
+    def scatter(stage, part, sib, half, rs):
+        for k in range(Z):
+            half[k] = part[c, k] + sib[k]
         for peer, device in z_peers:
-            @pl.when(peer < OWNERS)
-            def _():
-                send(stage, half.at[peer], rs.at[z], device)
-
-        @pl.when(z < OWNERS)
-        def _():
-            rs[z] = half[z]
-
-    def gather(stage, own, dst):
-        @pl.when(z < OWNERS)
-        def _():
-            dst[mine + z] = own[...]
-            for _, device in z_peers:
-                send(stage, own, dst.at[mine + z], device)
+            send(stage, half.at[peer], rs.at[z], device)
+        rs[z] = half[z]
+
+    def gather(stage, rs_stage, rs, own, dst):
+        received(rs_stage, rs.at[pl.ds(0, Z - 1)])
+        own[...] = total(rs, Z)
+        for _, device in z_peers:
+            send(stage, own, dst.at[c, z], device)
+        dst[c, z] = own[...]
 
     def gathered(stage, dst):
-        @pl.when(z < OWNERS)
-        def _():
-            received(stage, dst.at[pl.ds(0, OWNERS - 1)])
-
-        @pl.when(z == OWNERS)
-        def _():
-            received(stage, dst.at[pl.ds(0, OWNERS)])
-
+        received(stage, dst.at[c, pl.ds(0, Z - 1)])
+
+    received(1, sg_sib)
+    scatter(7, sg_part, sg_sib, sg_half, rs_g)
     received(0, sd_sib)
     reduce_first(2, sd_part[c] + sd_sib[...], msg_d, z1_d, x1_d)
-    received(1, sg_sib)
-    for i in range(OWNERS):
-        sg_half[i] = sg_part[mine + i] + sg_sib[i]
-    scatter(7, sg_half, rs_g)
+    send(20, full_d.at[pl.ds(pl.multiple_of((1 - c) * d_half, LANES), d_half)], md_in, sibling)
+    send(21, full_g.at[pl.ds(pl.multiple_of((1 - c) * g_half, LANES), g_half)], mg_in, sibling)
 
     received(20, md_in)
     for b in range(blocks):
@@ -233,19 +234,39 @@
         md[d_half : 2 * d_half, cols] = mid
         md[2 * d_half :, cols] = lo
     received(21, mg_in)
-    for b in range(OWNERS):
+    for b in range(HALF):
         parts = split3(full_g[pl.ds(pl.multiple_of(c * g_half + b * LANES, LANES), LANES), :] + mg_in[pl.ds(b * LANES, LANES), :])
         for i in range(3):
             mg[i, pl.ds(b * LANES, LANES), :] = parts[i]
 
+    gather(8, 7, rs_g, own_g, sg)
+
     reduce_second(2, z1_d, x1_d, mid_d, z2_d, x2_d)
 
-    @pl.when(z < OWNERS)
-    def _():
-        received(7, rs_g.at[pl.ds(0, Z - 1)])
-        own_g[...] = total(rs_g, Z)
-
-    gather(8, own_g, sg)
+    gathered(8, sg)
+    tiles = [jnp.concatenate([tile_of(sg, c, i) for i in range(b, min(b + 2, HALF))], axis=1) for b in range(0, HALF, 2)]
+    sfg_sum = None
+    for b, tile in enumerate(tiles):
+        rows = pl.ds(b * BLOCK, tile.shape[1])
+        term = dot6(rows3(tile), [mg[i, rows, :] for i in range(3)], NN)
+        sfg_sum = term if sfg_sum is None else sfg_sum + term
+    for i in range(2):
+        sfg[i] = sfg_sum[:, i * LANES : (i + 1) * LANES]
+    send(12, sfg.at[1 - c], sfg_sib, sibling)
+    gram_sum = None
+    for tile in tiles:
+        pad = jnp.zeros((LANES - RANK, tile.shape[1]), F32)
+        term = dot6(rows3(tile), split3(jnp.concatenate([tile, pad], axis=0)), NT)
+        gram_sum = term if gram_sum is None else gram_sum + term
+    packed = gram_sum[0:8]
+    for i in range(1, 4):
+        packed = packed + pltpu.roll(gram_sum[8 * i : 8 * i + 8], RANK * i, 1)
+    gram_own[...] = packed
+    send(22, gram_own, gram_sib, sibling)
+
+    received(12, sfg_sib)
+    received(22, gram_sib)
+    reduce_first(13, jnp.concatenate([sfg[c] + sfg_sib[...], gram_own[...] + gram_sib[...]], axis=0), msg_g, z1_g, x1_g)
 
     reduce_third(2, z2_d, x2_d, sd)
 
@@ -263,71 +284,44 @@
         a = dot(stacked, md[0 : 2 * d_half, cols], NN)
         small = dot(hi, md[2 * d_half :, cols], NN) + a[2 * RANK :]
         term = a[:RANK] + (a[RANK : 2 * RANK] + small)
-        sfd[2 * b] = term[:, :LANES]
-        sfd[2 * b + 1] = term[:, LANES:]
-    send(9, sfd.at[pl.ds(other, OWNERS)], sfd_sib, sibling)
-
-    gathered(8, sg)
-    send(10, sg.at[pl.ds(mine, OWNERS)], sg.at[pl.ds(mine, OWNERS)], sibling)
-    sfg_sum = None
-    gram_sum = None
-    for b in range(0, OWNERS, 2):
-        n = min(2, OWNERS - b)
-        rows = pl.ds(b * LANES, n * LANES)
-        tile = jnp.concatenate([sg[mine + b + i] for i in range(n)], axis=1)
-        term = dot6(rows3(tile), [mg[i, rows, :] for i in range(3)], NN)
-        sfg_sum = term if sfg_sum is None else sfg_sum + term
-        pad = jnp.zeros((LANES - RANK, n * LANES), F32)
-        term = dot_high(tile, jnp.concatenate([tile, pad], axis=0), NT)
-        gram_sum = term if gram_sum is None else gram_sum + term
-    packed = gram_sum[0:8]
-    for i in range(1, 4):
-        packed = packed + pltpu.roll(gram_sum[8 * i : 8 * i + 8], RANK * i, 1)
-    for i in range(2):
-        sfg[i, 0:RANK] = sfg_sum[:, i * LANES : (i + 1) * LANES]
-        sfg[i, RANK:] = packed
-    send(12, sfg.at[1 - c], sfg_sib, sibling)
+        put_tile(sfd, 2 * b, term[:, :LANES])
+        put_tile(sfd, 2 * b + 1, term[:, LANES:])
+    send(9, sfd.at[1 - c], sfd_sib, sibling)
 
     received(9, sfd_sib)
-    for i in range(OWNERS):
-        sfd_half[i] = sfd[mine + i] + sfd_sib[i]
-    scatter(11, sfd_half, rs_d)
-
-    received(12, sfg_sib)
-    reduce_first(13, sfg[c] + sfg_sib[...], msg_g, z1_g, x1_g)
+    scatter(11, sfd, sfd_sib, sfd_half, rs_d)
+    send(10, sg.at[c], sg.at[c], sibling)
 
     received(6, sd.at[1 - c])
     sketch_d = jnp.concatenate([sd[0], sd[1]], axis=1)
     pad = jnp.zeros((LANES - RANK, BLOCK), F32)
-    lower_d, inv_d = eliminate(dot_high(sketch_d, jnp.concatenate([sketch_d, pad], axis=0), NT))
-
-    @pl.when(z < OWNERS)
-    def _():
-        received(11, rs_d.at[pl.ds(0, Z - 1)])
-        own_d[...] = dot_high(lower_d, total(rs_d, Z), NN) * (inv_d * (1.0 / 16.0))
-
-    gather(18, own_d, co_d)
-    left_d[...] = jnp.transpose(left_six(dot_high(lower_d, sketch_d, NN)))
+    lower_d, upper_d, inv_d = eliminate(dot6(rows3(sketch_d), split3(jnp.concatenate([sketch_d, pad], axis=0)), NT))
+    solved = dot(left_lanes(lower_d), right_six(sketch_d), NN) * (inv_d * (1.0 / 16.0))
+    left_d[...] = jnp.transpose(left_six(dot(left_lanes(upper_d), right_six(solved), NN)))
 
     gram_packed = reduce_second(13, z1_g, x1_g, mid_g, z2_g, x2_g)
+
+    gather(18, 11, rs_d, own_d, co_d)
+
     lane = lax.broadcasted_iota(jnp.int32, (8, LANES), 1)
     gram_g = jnp.concatenate(
         [jnp.where(lane < RANK, gram_packed if i == 0 else pltpu.roll(gram_packed, LANES - RANK * i, 1), 0.0) for i in range(4)],
         axis=0,
     )
-    lower_g, inv_g = eliminate(gram_g)
-    received(10, sg.at[pl.ds(other, OWNERS)])
-    for i in range(2 * OWNERS):
-        left_g[pl.ds(i * LANES, LANES), :] = jnp.transpose(left_six(dot_high(lower_g, sg[i], NN)))
-
+    lower_g, _, inv_g = eliminate(gram_g)
+    lower_g = left_lanes(lower_g)
+    received(10, sg.at[1 - c])
+    for i in range(HALF):
+        tile = jnp.concatenate([tile_of(sg, j // HALF, j % HALF) for j in (2 * i, 2 * i + 1)], axis=1)
+        left_g[pl.ds(i * BLOCK, BLOCK), :] = jnp.transpose(left_six(dot(lower_g, right_six(tile), NN)))
+
+    reduce_third(13, z2_g, x2_g, sum_g)
     gathered(18, co_d)
-    send(19, co_d.at[pl.ds(mine, OWNERS)], co_d.at[pl.ds(mine, OWNERS)], sibling)
-
-    reduce_third(13, z2_g, x2_g, sum_g)
+    send(19, co_d.at[c], co_d.at[c], sibling)
     received(17, sum_g.at[1 - c])
-    coeff = dot_high(lower_g, jnp.concatenate([sum_g[0], sum_g[1]], axis=1), NN) * (inv_g * (1.0 / 16.0))
+    coeff = dot(lower_g, right_six(jnp.concatenate([sum_g[0], sum_g[1]], axis=1)), NN) * (inv_g * (1.0 / 16.0))
     right_g[...] = right_six(coeff)
-    received(19, co_d.at[pl.ds(other, OWNERS)])
+    received(19, co_d.at[1 - c])
     coeff_d[...] = co_d[...]
 
     sent(0, sd_sib)
@@ -336,6 +330,7 @@
     sent(21, mg_in)
     sent(9, sfd_sib)
     sent(12, sfg_sib)
+    sent(22, gram_sib)
     sent(10, sg_sib)
     sent(19, sg_sib)
     for base, z1, x1, z2, x2, full in (
@@ -347,15 +342,8 @@
         sent(base + 2, z2.at[pl.ds(0, Z - 1)])
         sent(base + 3, x2.at[pl.ds(0, XY - 1)])
         sent(base + 4, full.at[0])
-    for scatter_stage, gather_stage, rs in ((7, 8, rs_g), (11, 18, rs_d)):
-        @pl.when(z < OWNERS)
-        def _():
-            sent(scatter_stage, rs.at[pl.ds(0, OWNERS - 1)])
-            sent(gather_stage, rs.at[pl.ds(0, Z - 1)])
-
-        @pl.when(z == OWNERS)
-        def _():
-            sent(scatter_stage, rs.at[pl.ds(0, OWNERS)])
+    for stage, rs in ((7, rs_g), (8, rs_g), (11, rs_d), (18, rs_d)):
+        sent(stage, rs.at[pl.ds(0, Z - 1)])
 
 
 def finish_kernel(full_g, full_d, left_g, right_g, left_d, coeff_d, ug_hbm, ng_hbm, ud_hbm, nd_hbm, ug, ng, ud, nd, sem):
@@ -373,7 +361,7 @@
         store(ug.at[part], ug_hbm.at[part])
         store(ng.at[part], ng_hbm.at[part])
         part = (slice(None), pl.ds(b * BLOCK, BLOCK))
-        right = right_six(jnp.concatenate([coeff_d[2 * b], coeff_d[2 * b + 1]], axis=1))
+        right = right_six(jnp.concatenate([tile_of(coeff_d, j // HALF, j % HALF) for j in (2 * b, 2 * b + 1)], axis=1))
         update = dot(left_d[...], right, NN)
         ud[part] = update
         nd[part] = full_d[part] - update
@@ -386,9 +374,10 @@
 def local(grad_gate, error_gate, query_gate, grad_down, error_down, query_down):
     gg, eg, gd, ed = grad_gate[0], error_gate[0], grad_down[0], error_down[0]
     ff, rows = gg.shape
-    tiles = ff // LANES
     vmem = pltpu.VMEM
     tile = (RANK, LANES)
+    half = (Z, HALF * CHUNK, LANES)
+    chunk, both = vmem(half[1:], F32), vmem((2, *half), F32)
 
     def stack(n, r=RANK):
         return vmem((n, r, LANES), F32)
@@ -400,17 +389,17 @@
         [vmem((ff, rows), BF16), vmem((ff, rows), F32), vmem((RANK, rows), F32)]
         + [vmem((rows, ff), BF16), vmem((rows, ff), F32), vmem((RANK, ff), F32)]
         + [vmem((ff // 2, rows), F32), vmem((rows // 2, ff), F32), vmem((3, ff // 2, rows), BF16), vmem((3 * rows // 2, ff), BF16)]
-        + [stack(tiles), stack(OWNERS), stack(OWNERS), stack(Z), stack(tiles)]
-        + [stack(2, RANK + 8), vmem((RANK + 8, LANES), F32)] + reduce_buffers(8)
+        + [both, vmem(half, F32), vmem(half, F32), vmem(half, F32), both]
+        + [stack(2), vmem(tile, F32), vmem((8, LANES), F32), vmem((8, LANES), F32)] + reduce_buffers(8)
         + [stack(2), vmem(tile, F32)] + reduce_buffers(0)
-        + [stack(tiles), stack(OWNERS), stack(OWNERS), stack(Z), vmem(tile, F32), vmem(tile, F32), stack(tiles)]
-        + [pltpu.SemaphoreType.DMA((6,)), pltpu.SemaphoreType.DMA((22,)), pltpu.SemaphoreType.DMA((22,))]
+        + [both, vmem(half, F32), vmem(half, F32), vmem(half, F32), chunk, chunk, both]
+        + [pltpu.SemaphoreType.DMA((6,)), pltpu.SemaphoreType.DMA((23,)), pltpu.SemaphoreType.DMA((23,))]
     )
     whole = pl.BlockSpec(memory_space=pltpu.VMEM)
     gate_shape, down_shape = (ff, rows), (rows, ff)
     shapes = [
         (gate_shape, F32), (down_shape, F32), ((ff, 6 * RANK), BF16), ((6 * RANK, rows), BF16),
-        ((rows, 6 * RANK), BF16), ((tiles, RANK, LANES), F32),
+        ((rows, 6 * RANK), BF16), ((2, *half), F32),
     ]
     inputs = [pltpu.with_memory_space_constraint(a, pltpu.HBM) for a in (gg, eg, query_gate, gd, ed, query_down)]
     middle = pl.pallas_call(

time: 46.7 us -> 43.6 us (0.934)
  Pallas kernels: 45.9 us -> 42.9 us
    pallas_call x1, Pallas kernels: 42.5 us -> 39.5 us  [local(): pl.pallas_call(exchange_kernel, out_shape=[pltpu.VMEM(shape, dtype) for s...]
where the time goes in v3:
time: 43.6 us
  Pallas kernels  42.9 us (98%)
  between operations  0.64 us (1%)
    pallas_call x1, Pallas kernels, local(): pl.pallas_call(exchange_kernel, out_shape=[pltpu.VMEM(shape, dtype) for s...  39.5 us
    pallas_call x1, Pallas kernels, local(): pl.pallas_call(finish_kernel, out_shape=[jax.ShapeDtypeStruct(shape, F32)...  3.42 us

profile of v3, /device:TPU:1, one launch (start us, length us, event | category | flops | bytes accessed | tf_op | source)
XLA Modules:
  0.0 43.6 jit_solution(5914405679971251680)
XLA Ops:
  0.6 39.5 %shard_map.93 = (f32[1792,256]{1,0:T(8,128)S(1)}, f32[256,1792]{1,0:T(8,128)S(1)}, bf16[1792,192]{1,0:T(8,128)(2,1)S(1)}, bf16[192,256]{1,0:T(8,128)(2,1)S(1)}, ...) custom-call(bf16[1792,256]{1,0:T(8,128)(2,1)} %bitcast.8, f32[1792,256]{1,0:T(8,128)} %bitcast.6, ...), custom_call_target="tpu_custom_call" | custom-call | tf_op jit(solution)/shard_map/pallas_call | solution.py:405
  40.1 3.4 %shard_map.94 = (f32[1792,256]{1,0:T(8,128)}, f32[1792,256]{1,0:T(8,128)}, f32[256,1792]{1,0:T(8,128)}, f32[256,1792]{1,0:T(8,128)}) custom-call(f32[1792,256]{1,0:T(8,128)S(1)} %get-tuple-element.14.full_g, f32[256,1792]{1,0:T(8,128)S(1)} %get-tuple-element.15.full_d, bf16[1792,192]{1,0:T(8,128)(2,1)S(1)} %get-tuple-element.16.left_g, ...), custom_call_target="tpu_custom_call" | custom-call | tf_op jit(solution)/shard_map/pallas_call | solution.py:415

commit v4 on v3

--- a/solution.py
+++ b/solution.py
@@ -54,10 +54,9 @@
     return jnp.concatenate([ref[half, k, CHUNK * i : CHUNK * (i + 1)] for k in range(Z)], axis=0)
 
 
-def put_tile(ref, j, tile):
-    i = CHUNK * (j % HALF)
+def put_tile(ref, half, i, tile):
     for k in range(Z):
-        ref[j // HALF, k, i : i + CHUNK] = tile[k * CHUNK : (k + 1) * CHUNK]
+        ref[half, k, CHUNK * i : CHUNK * (i + 1)] = tile[k * CHUNK : (k + 1) * CHUNK]
 
 
 def total(ref, n):
@@ -103,7 +102,7 @@
     full_g, full_d, left_g, right_g, left_d, coeff_d,
     gg, eg, qg, gd, ed, qd, mg_in, md_in, mg, md,
     sg_part, sg_sib, sg_half, rs_g, sg,
-    sfg, sfg_sib, gram_own, gram_sib, msg_g, z1_g, x1_g, mid_g, z2_g, x2_g, sum_g,
+    sfg, sfg_sib, gram_own, gram_sib, gram_pair, gram_all, msg_g, z1_g, x1_g, mid_g, z2_g, x2_g, sum_g,
     sd_part, sd_sib, msg_d, z1_d, x1_d, mid_d, z2_d, x2_d, sd,
     sfd, sfd_sib, sfd_half, rs_d, own_g, own_d, co_d,
     load_sem, send_sem, recv_sem,
@@ -161,8 +160,8 @@
         block = gg[rows, :].astype(F32) + eg[rows, :]
         full_g[rows, :] = block
         term = dot6(qg3, split3(block), NT)
-        put_tile(sg_part, 2 * b, term[:, :LANES])
-        put_tile(sg_part, 2 * b + 1, term[:, LANES:])
+        for j, tile in ((2 * b, term[:, :LANES]), (2 * b + 1, term[:, LANES:])):
+            put_tile(sg_part, j // HALF, j % HALF, tile)
 
     pl.semaphore_wait(barrier, 1 + len(z_peers) + len(xy_peers))
 
@@ -188,11 +187,10 @@
             send(base + 3, mid.at[pl.ds(0, 16)], x2.at[t], device)
         received(base + 1, x1.at[pl.ds(0, XY - 1)])
         high = total(x1, XY)
-        mid[16:32] = high[0:16]
-        z2[z] = high[0:16]
+        mid[16:32] = high
+        z2[z] = high
         for _, device in z_peers:
             send(base + 2, mid.at[pl.ds(16, 16)], z2.at[z], device)
-        return high[16:]
 
     def reduce_third(base, z2, x2, full):
         received(base + 2, z2.at[pl.ds(0, Z - 1)])
@@ -265,8 +263,12 @@
     send(22, gram_own, gram_sib, sibling)
 
     received(12, sfg_sib)
+    reduce_first(13, sfg[c] + sfg_sib[...], msg_g, z1_g, x1_g)
     received(22, gram_sib)
-    reduce_first(13, jnp.concatenate([sfg[c] + sfg_sib[...], gram_own[...] + gram_sib[...]], axis=0), msg_g, z1_g, x1_g)
+    gram_pair[...] = gram_own[...] + gram_sib[...]
+    gram_all[t] = gram_pair[...]
+    for device in xy_peers:
+        send(23, gram_pair, gram_all.at[t], device)
 
     reduce_third(2, z2_d, x2_d, sd)
 
@@ -279,18 +281,23 @@
         ],
         axis=0,
     )
-    for b in range(blocks):
-        cols = pl.ds(b * BLOCK, BLOCK)
-        a = dot(stacked, md[0 : 2 * d_half, cols], NN)
-        small = dot(hi, md[2 * d_half :, cols], NN) + a[2 * RANK :]
-        term = a[:RANK] + (a[RANK : 2 * RANK] + small)
-        put_tile(sfd, 2 * b, term[:, :LANES])
-        put_tile(sfd, 2 * b + 1, term[:, LANES:])
+
+    def product(half):
+        for i in range(0, HALF, 2):
+            n = min(2, HALF - i)
+            cols = pl.ds(pl.multiple_of((half * HALF + i) * LANES, LANES), n * LANES)
+            a = dot(stacked, md[0 : 2 * d_half, cols], NN)
+            small = dot(hi, md[2 * d_half :, cols], NN) + a[2 * RANK :]
+            term = a[:RANK] + (a[RANK : 2 * RANK] + small)
+            for k in range(n):
+                put_tile(sfd, half, i + k, term[:, k * LANES : (k + 1) * LANES])
+
+    product(1 - c)
     send(9, sfd.at[1 - c], sfd_sib, sibling)
+    product(c)
 
     received(9, sfd_sib)
     scatter(11, sfd, sfd_sib, sfd_half, rs_d)
-    send(10, sg.at[c], sg.at[c], sibling)
 
     received(6, sd.at[1 - c])
     sketch_d = jnp.concatenate([sd[0], sd[1]], axis=1)
@@ -299,10 +306,13 @@
     solved = dot(left_lanes(lower_d), right_six(sketch_d), NN) * (inv_d * (1.0 / 16.0))
     left_d[...] = jnp.transpose(left_six(dot(left_lanes(upper_d), right_six(solved), NN)))
 
-    gram_packed = reduce_second(13, z1_g, x1_g, mid_g, z2_g, x2_g)
+    reduce_second(13, z1_g, x1_g, mid_g, z2_g, x2_g)
+    send(10, sg.at[c], sg.at[c], sibling)
 
     gather(18, 11, rs_d, own_d, co_d)
 
+    received(23, gram_all.at[pl.ds(0, XY - 1)])
+    gram_packed = total(gram_all, XY)
     lane = lax.broadcasted_iota(jnp.int32, (8, LANES), 1)
     gram_g = jnp.concatenate(
         [jnp.where(lane < RANK, gram_packed if i == 0 else pltpu.roll(gram_packed, LANES - RANK * i, 1), 0.0) for i in range(4)],
@@ -331,6 +341,7 @@
     sent(9, sfd_sib)
     sent(12, sfg_sib)
     sent(22, gram_sib)
+    sent(23, gram_all.at[pl.ds(0, XY - 1)])
     sent(10, sg_sib)
     sent(19, sg_sib)
     for base, z1, x1, z2, x2, full in (
@@ -382,18 +393,18 @@
     def stack(n, r=RANK):
         return vmem((n, r, LANES), F32)
 
-    def reduce_buffers(extra):
-        return [vmem((RANK + extra, LANES), F32), stack(Z, 16), stack(XY, 16 + extra), vmem(tile, F32), stack(Z, 16), stack(XY, 16), stack(2)]
+    def reduce_buffers():
+        return [vmem(tile, F32), stack(Z, 16), stack(XY, 16), vmem(tile, F32), stack(Z, 16), stack(XY, 16), stack(2)]
 
     scratch = (
         [vmem((ff, rows), BF16), vmem((ff, rows), F32), vmem((RANK, rows), F32)]
         + [vmem((rows, ff), BF16), vmem((rows, ff), F32), vmem((RANK, ff), F32)]
         + [vmem((ff // 2, rows), F32), vmem((rows // 2, ff), F32), vmem((3, ff // 2, rows), BF16), vmem((3 * rows // 2, ff), BF16)]
         + [both, vmem(half, F32), vmem(half, F32), vmem(half, F32), both]
-        + [stack(2), vmem(tile, F32), vmem((8, LANES), F32), vmem((8, LANES), F32)] + reduce_buffers(8)
-        + [stack(2), vmem(tile, F32)] + reduce_buffers(0)
+        + [stack(2), vmem(tile, F32), vmem((8, LANES), F32), vmem((8, LANES), F32), vmem((8, LANES), F32), stack(XY, 8)] + reduce_buffers()
+        + [stack(2), vmem(tile, F32)] + reduce_buffers()
         + [both, vmem(half, F32), vmem(half, F32), vmem(half, F32), chunk, chunk, both]
-        + [pltpu.SemaphoreType.DMA((6,)), pltpu.SemaphoreType.DMA((23,)), pltpu.SemaphoreType.DMA((23,))]
+        + [pltpu.SemaphoreType.DMA((6,)), pltpu.SemaphoreType.DMA((24,)), pltpu.SemaphoreType.DMA((24,))]
     )
     whole = pl.BlockSpec(memory_space=pltpu.VMEM)
     gate_shape, down_shape = (ff, rows), (rows, ff)

time: 43.6 us -> 43.5 us (level)
  no operation moved by 1% of the time
where the time goes in v4:
time: 43.5 us; the launch traced here: 43.4 us
  Pallas kernels  42.8 us (98%)
  between operations  0.64 us (1%)
    pallas_call x1, Pallas kernels, local(): pl.pallas_call(exchange_kernel, out_shape=[pltpu.VMEM(shape, dtype) for s...  39.4 us
    pallas_call x1, Pallas kernels, local(): pl.pallas_call(finish_kernel, out_shape=[jax.ShapeDtypeStruct(shape, F32)...  3.42 us

profile of v4, /device:TPU:1, one launch (start us, length us, event | category | flops | bytes accessed | tf_op | source)
XLA Modules:
  0.0 43.4 jit_solution(18217871546266365291)
XLA Ops:
  0.6 39.4 %shard_map.93 = (f32[1792,256]{1,0:T(8,128)S(1)}, f32[256,1792]{1,0:T(8,128)S(1)}, bf16[1792,192]{1,0:T(8,128)(2,1)S(1)}, bf16[192,256]{1,0:T(8,128)(2,1)S(1)}, ...) custom-call(bf16[1792,256]{1,0:T(8,128)(2,1)} %bitcast.8, f32[1792,256]{1,0:T(8,128)} %bitcast.6, ...), custom_call_target="tpu_custom_call" | custom-call | tf_op jit(solution)/shard_map/pallas_call | solution.py:416
  40.0 3.4 %shard_map.94 = (f32[1792,256]{1,0:T(8,128)}, f32[1792,256]{1,0:T(8,128)}, f32[256,1792]{1,0:T(8,128)}, f32[256,1792]{1,0:T(8,128)}) custom-call(f32[1792,256]{1,0:T(8,128)S(1)} %get-tuple-element.14.full_g, f32[256,1792]{1,0:T(8,128)S(1)} %get-tuple-element.15.full_d, bf16[1792,192]{1,0:T(8,128)(2,1)S(1)} %get-tuple-element.16.left_g, ...), custom_call_target="tpu_custom_call" | custom-call | tf_op jit(solution)/shard_map/pallas_call | solution.py:426

commit v5 on v4

--- a/solution.py
+++ b/solution.py
@@ -104,7 +104,7 @@
     sg_part, sg_sib, sg_half, rs_g, sg,
     sfg, sfg_sib, gram_own, gram_sib, gram_pair, gram_all, msg_g, z1_g, x1_g, mid_g, z2_g, x2_g, sum_g,
     sd_part, sd_sib, msg_d, z1_d, x1_d, mid_d, z2_d, x2_d, sd,
-    sfd, sfd_sib, sfd_half, rs_d, own_g, own_d, co_d,
+    sfd, sfd_sib, sfd_half, rs_d, own_g, own_d,
     load_sem, send_sem, recv_sem,
 ):
     dp, t = lax.axis_index("dp"), lax.axis_index("tensor")
@@ -309,7 +309,7 @@
     reduce_second(13, z1_g, x1_g, mid_g, z2_g, x2_g)
     send(10, sg.at[c], sg.at[c], sibling)
 
-    gather(18, 11, rs_d, own_d, co_d)
+    gather(18, 11, rs_d, own_d, coeff_d)
 
     received(23, gram_all.at[pl.ds(0, XY - 1)])
     gram_packed = total(gram_all, XY)
@@ -326,13 +326,12 @@
         left_g[pl.ds(i * BLOCK, BLOCK), :] = jnp.transpose(left_six(dot(lower_g, right_six(tile), NN)))
 
     reduce_third(13, z2_g, x2_g, sum_g)
-    gathered(18, co_d)
-    send(19, co_d.at[c], co_d.at[c], sibling)
+    gathered(18, coeff_d)
+    send(19, coeff_d.at[c], coeff_d.at[c], sibling)
     received(17, sum_g.at[1 - c])
     coeff = dot(lower_g, right_six(jnp.concatenate([sum_g[0], sum_g[1]], axis=1)), NN) * (inv_g * (1.0 / 16.0))
     right_g[...] = right_six(coeff)
-    received(19, co_d.at[1 - c])
-    coeff_d[...] = co_d[...]
+    received(19, coeff_d.at[1 - c])
 
     sent(0, sd_sib)
     sent(1, sg_sib)
@@ -403,7 +402,7 @@
         + [both, vmem(half, F32), vmem(half, F32), vmem(half, F32), both]
         + [stack(2), vmem(tile, F32), vmem((8, LANES), F32), vmem((8, LANES), F32), vmem((8, LANES), F32), stack(XY, 8)] + reduce_buffers()
         + [stack(2), vmem(tile, F32)] + reduce_buffers()
-        + [both, vmem(half, F32), vmem(half, F32), vmem(half, F32), chunk, chunk, both]
+        + [both, vmem(half, F32), vmem(half, F32), vmem(half, F32), chunk, chunk]
         + [pltpu.SemaphoreType.DMA((6,)), pltpu.SemaphoreType.DMA((24,)), pltpu.SemaphoreType.DMA((24,))]
     )
     whole = pl.BlockSpec(memory_space=pltpu.VMEM)

time: 43.5 us -> 43.5 us (level)
  no operation moved by 1% of the time
where the time goes in v5:
time: 43.5 us; the launch traced here: 43.4 us
  Pallas kernels  42.8 us (98%)
  between operations  0.64 us (1%)
    pallas_call x1, Pallas kernels, local(): pl.pallas_call(exchange_kernel, out_shape=[pltpu.VMEM(shape, dtype) for s...  39.3 us
    pallas_call x1, Pallas kernels, local(): pl.pallas_call(finish_kernel, out_shape=[jax.ShapeDtypeStruct(shape, F32)...  3.41 us

profile of v5, /device:TPU:1, one launch (start us, length us, event | category | flops | bytes accessed | tf_op | source)
XLA Modules:
  0.0 43.4 jit_solution(9449934262733522296)
XLA Ops:
  0.6 39.3 %shard_map.93 = (f32[1792,256]{1,0:T(8,128)S(1)}, f32[256,1792]{1,0:T(8,128)S(1)}, bf16[1792,192]{1,0:T(8,128)(2,1)S(1)}, bf16[192,256]{1,0:T(8,128)(2,1)S(1)}, ...) custom-call(bf16[1792,256]{1,0:T(8,128)(2,1)} %bitcast.8, f32[1792,256]{1,0:T(8,128)} %bitcast.6, ...), custom_call_target="tpu_custom_call" | custom-call | tf_op jit(solution)/shard_map/pallas_call | solution.py:415
  40.0 3.4 %shard_map.94 = (f32[1792,256]{1,0:T(8,128)}, f32[1792,256]{1,0:T(8,128)}, f32[256,1792]{1,0:T(8,128)}, f32[256,1792]{1,0:T(8,128)}) custom-call(f32[1792,256]{1,0:T(8,128)S(1)} %get-tuple-element.14.full_g, f32[256,1792]{1,0:T(8,128)S(1)} %get-tuple-element.15.full_d, bf16[1792,192]{1,0:T(8,128)(2,1)S(1)} %get-tuple-element.16.left_g, ...), custom_call_target="tpu_custom_call" | custom-call | tf_op jit(solution)/shard_map/pallas_call | solution.py:425
